TPU v7x, 256 devices: a whole 4x4x8 slice. The times are simulated.
256 devices in a mesh: dp: 8 (over x_hi, y), mp: 32 (over z, x_lo, core).
Axes of the slice: x: 4 (x_hi: 2, x_lo: 2; x = x_hi * 2 + x_lo), y: 4, z: 8, core: 2. Of those that a mesh axis runs over, the one named last changes fastest.
Arguments:
- tokens: bfloat16 [6144, 4096], P('dp', 'mp'), may hold values from -6 to 6
- cotangent: bfloat16 [6144, 4096], P('dp', 'mp'), may hold values from -6 to 6
- up_tiles: bfloat16 [384, 256, 256], P('mp'), may hold values from -0.1875 to 0.1875
- up_rows: int32 [384], P('mp'), may hold values from 0 to 15
- up_columns: int32 [384], P('mp'), may hold values from 0 to 63, as said below
- up_counts: int32 [32], P('mp'), may hold values from 6 to 12, as said below
- down_tiles: bfloat16 [384, 256, 256], P('mp'), may hold values from -0.09375 to 0.09375
- down_rows: int32 [384], P('mp'), may hold values from 0 to 63, as said below
- down_columns: int32 [384], P('mp'), may hold values from 0 to 15
- down_counts: int32 [32], P('mp'), may hold values from 6 to 12, as said below
Outputs:
- mixed: bfloat16 [6144, 4096], P('dp', 'mp')
- token_grads: bfloat16 [6144, 4096], P('dp', 'mp')
- up_grads: float32 [384, 256, 256], P('mp', 'dp')
- down_grads: float32 [384, 256, 256], P('mp', 'dp')
Inputs may be any that keep to these rules, and one draw needn't show every extreme that they name: For the up slots of index j of mp, up_columns lies among that index's hidden blocks j * 2 to (j + 1) * 2 - 1; the live slots of one index name distinct blocks. `up_counts`: some index of mp has exactly 12 live up slots in every draw. For the down slots of index j of mp, down_rows lies among that index's hidden blocks j * 2 to (j + 1) * 2 - 1; the live slots of one index name distinct blocks. `down_counts`: some index of mp has exactly 12 live down slots in every draw.
All inputs are finite; a program needn't handle non-finite values.
Results may differ from a plain program's by a relative error of at most 0.023.
Values may be sent and summed in bfloat16 or wider, within the bound.
A program may use at most 128 MiB of HBM per device.

v0:
```python
import math

import jax
import jax.numpy as jnp
from jax import lax
from jax.sharding import PartitionSpec as P

D = 4096
FF = 16384
BLK = 256
DB = 16


def gelu_value(values):
    return 0.5 * values * (1.0 + jax.scipy.special.erf(values * 0.7071067811865476))


def gelu_slope(values):
    return (
        0.5 * (1.0 + jax.scipy.special.erf(values * 0.7071067811865476))
        + values * jnp.exp(-0.5 * values * values) * 0.3989422804014327
    )


def pick_table(labels, count):
    return (labels[:, None] == jnp.arange(count, dtype=jnp.int32)[None, :]).astype(jnp.float32)


def local(
    tokens,
    cotangent,
    up_tiles,
    up_rows,
    up_columns,
    up_counts,
    down_tiles,
    down_rows,
    down_columns,
    down_counts,
):
    highest = lax.Precision.HIGHEST
    tok_rows = tokens.shape[0]
    model_size = lax.axis_size("mp")
    hidden_blocks = FF // (BLK * model_size)
    slot_count = up_tiles.shape[0]
    device_place = lax.axis_index("mp")
    grad_scale = 1.0 / math.sqrt(tok_rows * lax.axis_size("dp"))
    slot_ids = jnp.arange(slot_count, dtype=jnp.int32)
    live_up = (slot_ids < up_counts[0]).astype(jnp.float32)
    live_down = (slot_ids < down_counts[0]).astype(jnp.float32)
    up_local = up_columns - device_place * hidden_blocks
    down_local = down_rows - device_place * hidden_blocks
    full_tokens = lax.all_gather(tokens, "mp", axis=1, tiled=True)
    token_gathered = full_tokens.reshape(tok_rows, DB, BLK)[:, up_rows]
    up_terms = (
        jnp.einsum("tsk,skn->tsn", token_gathered, up_tiles, preferred_element_type=jnp.float32)
        * live_up[None, :, None]
    )
    pre_hidden = jnp.einsum(
        "tsn,sc->tcn", up_terms, pick_table(up_local, hidden_blocks), precision=highest
    ).reshape(tok_rows, hidden_blocks * BLK)
    active = gelu_value(pre_hidden).astype(jnp.bfloat16)
    act_gathered = active.reshape(tok_rows, hidden_blocks, BLK)[:, down_local]
    down_terms = (
        jnp.einsum("tsk,skn->tsn", act_gathered, down_tiles, preferred_element_type=jnp.float32)
        * live_down[None, :, None]
    )
    partial_out = jnp.einsum(
        "tsn,sd->tdn", down_terms, pick_table(down_columns, DB), precision=highest
    ).reshape(tok_rows, D)
    mixed = lax.psum_scatter(
        partial_out.astype(jnp.bfloat16), "mp", scatter_dimension=1, tiled=True
    )
    full_cot = lax.all_gather(cotangent, "mp", axis=1, tiled=True)
    cot_gathered = full_cot.reshape(tok_rows, DB, BLK)[:, down_columns]
    back_terms = (
        jnp.einsum("tsn,skn->tsk", cot_gathered, down_tiles, preferred_element_type=jnp.float32)
        * live_down[None, :, None]
    )
    back_hidden = jnp.einsum(
        "tsk,sc->tck", back_terms, pick_table(down_local, hidden_blocks), precision=highest
    ).reshape(tok_rows, hidden_blocks * BLK)
    slope = (back_hidden * gelu_slope(pre_hidden)).astype(jnp.bfloat16)
    down_grad = (
        jnp.einsum("tsk,tsn->skn", act_gathered, cot_gathered, preferred_element_type=jnp.float32)
        * live_down[:, None, None]
        * grad_scale
    )
    slope_gathered = slope.reshape(tok_rows, hidden_blocks, BLK)[:, up_local]
    input_terms = (
        jnp.einsum("tsn,skn->tsk", slope_gathered, up_tiles, preferred_element_type=jnp.float32)
        * live_up[None, :, None]
    )
    partial_back = jnp.einsum(
        "tsk,sd->tdk", input_terms, pick_table(up_rows, DB), precision=highest
    ).reshape(tok_rows, D)
    token_grads = lax.psum_scatter(
        partial_back.astype(jnp.bfloat16), "mp", scatter_dimension=1, tiled=True
    )
    up_grad = (
        jnp.einsum(
            "tsk,tsn->skn", token_gathered, slope_gathered, preferred_element_type=jnp.float32
        )
        * live_up[:, None, None]
        * grad_scale
    )
    up_grads, down_grads = (
        lax.psum_scatter(
            up_grad.astype(jnp.bfloat16), "dp", scatter_dimension=1, tiled=True
        ).astype(jnp.float32),
        lax.psum_scatter(
            down_grad.astype(jnp.bfloat16), "dp", scatter_dimension=1, tiled=True
        ).astype(jnp.float32),
    )
    return (mixed, token_grads, up_grads, down_grads)


def solution(mesh):
    return jax.shard_map(
        local,
        mesh=mesh,
        in_specs=(
            P("dp", "mp"),
            P("dp", "mp"),
            P("mp", None, None),
            P("mp"),
            P("mp"),
            P("mp"),
            P("mp", None, None),
            P("mp"),
            P("mp"),
            P("mp"),
        ),
        out_specs=(P("dp", "mp"), P("dp", "mp"), P("mp", "dp", None), P("mp", "dp", None)),
        check_vma=False,
    )
```

profile of v0, /device:TPU:8, one launch (start us, length us, event | category | flops | bytes accessed | tf_op | source)
XLA Modules:
  0.0 638.7 jit_solution(5349178348583614887)
XLA Ops:
  14.3 69.3 %all-gather.5.cloned.1.call-done = bf16[768,4096]{0,1:T(8,128)(2,1)} async-done(((bf16[768,128]{0,1:T(8,128)(2,1)}), bf16[768,4096]{0,1:T(8,128)(2,1)}) %all-gather.5.cloned.1.call-update) | async-done | bytes 6291472 | tf_op jit(solution)/shard_map/all_gather | solution.py:74
  83.6 8.7 %copy.50 = bf16[768,16,256]{2,0,1:T(8,128)(2,1)} copy(bf16[768,16,256]{0,2,1:T(8,128)(2,1)} %bitcast.98) | data formatting | bytes 12582912 | tf_op jit(solution)/shard_map/reshape | solution.py:75
  92.3 63.8 %all-gather.3.cloned.1.call-done = bf16[768,4096]{0,1:T(8,128)(2,1)} async-done(((bf16[768,128]{0,1:T(8,128)(2,1)}), bf16[768,4096]{0,1:T(8,128)(2,1)}) %all-gather.3.cloned.1.call-update) | async-done | bytes 6291472 | tf_op jit(solution)/shard_map/all_gather | solution.py:53
  156.1 8.5 %copy.45 = bf16[768,16,256]{2,0,1:T(8,128)(2,1)} copy(bf16[768,16,256]{0,2,1:T(8,128)(2,1)} %bitcast.99) | data formatting | bytes 12582912 | tf_op jit(solution)/shard_map/reshape | solution.py:54
  164.6 6.0 gather_fusion.2
  170.6 3.8 multiply_bitcast_fusion.1
  174.4 10.0 %fusion.2 = f32[2,768,256]{2,0,1:T(2,128)} fusion(f32[768,12,256]{2,0,1:T(8,128)S(1)} %multiply_bitcast_fusion.1, s32[12]{0:T(128)S(1)} %get-tuple-element.11), kind=kOutput, calls=%fused_computation.6 | convolution fusion | flops 56623128 | bytes 11010096 | tf_op jit(solution)/shard_map/tsk,sc->tck/dot_general | solution.py:80
  184.4 5.9 gather_fusion
  190.3 3.7 multiply_bitcast_fusion.3
  194.0 9.3 %fusion.6 = f32[2,768,256]{2,0,1:T(2,128)S(1)} fusion(f32[768,12,256]{2,0,1:T(8,128)S(1)} %multiply_bitcast_fusion.3, s32[12]{0:T(128)S(1)} %get-tuple-element.5), kind=kOutput, calls=%fused_computation.10 | convolution fusion | flops 56623128 | bytes 11010096 | tf_op jit(solution)/shard_map/tsn,sc->tcn/dot_general | solution.py:59
  204.1 3.1 gather_fusion.3
  207.3 6.7 %multiply_convert_fusion.1 = bf16[12,256,256]{2,1,0:T(8,128)(2,1)} fusion(bf16[12,768,256]{2,1,0:T(8,128)(2,1)} %gather_fusion.3, bf16[12,768,256]{2,1,0:T(8,128)(2,1)} %gather_fusion, f32[12]{0:T(128)S(1)} %compare_convert_fusion.1), kind=kOutput, calls=%fused_computation.33 | convolution fusion | flops 1210318848 | bytes 11010096 | tf_op jit(solution)/shard_map/tsk,tsn->skn/dot_general | solution.py:101
  214.0 3.2 gather_fusion.1
  217.3 6.6 %multiply_convert_fusion = bf16[12,256,256]{2,1,0:T(8,128)(2,1)} fusion(bf16[12,768,256]{2,1,0:T(8,128)(2,1)} %gather_fusion.2, bf16[12,768,256]{2,1,0:T(8,128)(2,1)} %gather_fusion.1, f32[12]{0:T(128)S(1)} %compare_convert_fusion), kind=kOutput, calls=%fused_computation.32 | convolution fusion | flops 1210318848 | bytes 11010096 | tf_op jit(solution)/shard_map/tsk,tsn->skn/dot_general | solution.py:85
  224.0 3.9 multiply_bitcast_fusion
  227.9 13.0 %convert_bitcast_fusion = bf16[768,16,256]{2,1,0:T(8,128)(2,1)} fusion(f32[768,12,256]{2,0,1:T(8,128)S(1)} %multiply_bitcast_fusion, s32[12]{0:T(128)S(1)} %copy-done.4), kind=kOutput, calls=%fused_computation.16 | convolution fusion | flops 456130752 | bytes 15728688 | tf_op jit(solution)/shard_map/tsk,sd->tdk/dot_general | solution.py:94
  240.9 9.1 %copy.63 = bf16[768,16,256]{0,2,1:T(8,128)(2,1)} copy(bf16[768,16,256]{2,1,0:T(8,128)(2,1)} %convert_bitcast_fusion) | data formatting | bytes 12582912
  251.5 3.7 multiply_bitcast_fusion.2
  255.2 13.1 %convert_bitcast_fusion.1 = bf16[768,16,256]{2,1,0:T(8,128)(2,1)} fusion(f32[768,12,256]{2,0,1:T(8,128)S(1)} %multiply_bitcast_fusion.2, s32[12]{0:T(128)S(1)} %copy-done.5), kind=kOutput, calls=%fused_computation.17 | convolution fusion | flops 456130752 | bytes 15728688 | tf_op jit(solution)/shard_map/tsn,sd->tdn/dot_general | solution.py:68
  268.3 9.2 %copy.62 = bf16[768,16,256]{0,2,1:T(8,128)(2,1)} copy(bf16[768,16,256]{2,1,0:T(8,128)(2,1)} %convert_bitcast_fusion.1) | data formatting | bytes 12582912
  277.6 14.8 %reduce-scatter.9.cloned.1.call-done = bf16[12,32,256]{2,1,0:T(8,128)(2,1)} async-done(((bf16[12,256,256]{2,1,0:T(8,128)(2,1)}), bf16[12,32,256]{2,1,0:T(8,128)(2,1)}) %reduce-scatter.9.cloned.1.call-update) | async-done | bytes 196624 | tf_op jit(solution)/shard_map/reduce_scatter | solution.py:108
  294.0 80.3 %reduce-scatter.11.cloned.1.call-done = bf16[12,32,256]{2,1,0:T(8,128)(2,1)} async-done(((bf16[12,256,256]{2,1,0:T(8,128)(2,1)}), bf16[12,32,256]{2,1,0:T(8,128)(2,1)}) %reduce-scatter.11.cloned.1.call-update) | async-done | bytes 196624 | tf_op jit(solution)/shard_map/reduce_scatter | solution.py:111
  376.0 126.8 %reduce-scatter.15.cloned.1.call-done = bf16[128,768]{1,0:T(8,128)(2,1)} async-done(((bf16[4096,768]{1,0:T(8,128)(2,1)}), bf16[128,768]{1,0:T(8,128)(2,1)}) %reduce-scatter.15.cloned.1.call-update) | async-done | bytes 196624
  504.6 125.5 %reduce-scatter.13.cloned.1.call-done = bf16[128,768]{1,0:T(8,128)(2,1)} async-done(((bf16[4096,768]{1,0:T(8,128)(2,1)}), bf16[128,768]{1,0:T(8,128)(2,1)}) %reduce-scatter.13.cloned.1.call-update) | async-done | bytes 196624
  (40 shorter events, 15.0 us)
Async XLA Ops:
  7.2 183.1 %copy-start = (bf16[12,256,256]{2,1,0:T(8,128)(2,1)S(1)}, bf16[12,256,256]{2,1,0:T(8,128)(2,1)}, u32[]{:S(2)}) copy-start(bf16[12,256,256]{2,1,0:T(8,128)(2,1)} %param.12) | copy-start | bytes 4718596
  7.2 76.4 %all-gather.5.cloned.1.call-start = ((), (), s32[]{:S(2)}) async-start(), calls=%async_computation.5 | async-start | bytes 6488064 | tf_op jit(solution)/shard_map/all_gather | solution.py:74
  9.1 147.0 %all-gather.3.cloned.1.call-start = ((), (), s32[]{:S(2)}) async-start(), calls=%async_computation.4 | async-start | bytes 6488064 | tf_op jit(solution)/shard_map/all_gather | solution.py:53
  10.9 281.4 %reduce-scatter.9.cloned.1.call-start = ((), (), s32[]{:S(2)}) async-start(), calls=%async_computation.6 | async-start | bytes 1769472 | tf_op jit(solution)/shard_map/reduce_scatter | solution.py:108
  164.6 6.0 copy-start.1
  194.0 9.3 %copy-start.3 = (f32[2,768,256]{2,0,1:T(2,128)S(1)}, f32[2,768,256]{2,0,1:T(2,128)}, u32[]{:S(2)}) copy-start(f32[2,768,256]{2,0,1:T(2,128)} %fusion.2) | copy-start | bytes 4718596
  214.0 160.4 %reduce-scatter.11.cloned.1.call-start = ((), (), s32[]{:S(2)}) async-start(), calls=%async_computation.7 | async-start | bytes 1769472 | tf_op jit(solution)/shard_map/reduce_scatter | solution.py:111
  223.9 4.0 copy-start.4
  224.0 278.9 %reduce-scatter.15.cloned.1.call-start = ((), (), s32[]{:S(2)}) async-start(), calls=%async_computation.9 | async-start | bytes 6488064
  250.0 1.4 copy-start.2
  250.1 5.1 copy-start.5
  250.1 380.0 %reduce-scatter.13.cloned.1.call-start = ((), (), s32[]{:S(2)}) async-start(), calls=%async_computation.8 | async-start | bytes 6488064
Sparse Core Ops, SparseCore 0:
  10.4 73.0 all-gather.4
  86.0 69.9 all-gather.2
  214.1 78.2 reduce-scatter.8
  296.7 77.5 reduce-scatter.10
  376.7 126.0 reduce-scatter.14
  505.3 124.8 reduce-scatter.12
where the time goes:
time: 640 us; the launch traced here: 639 us
  waiting for transfers between devices  481 us (75%)
  matrix products  73.8 us (12%)
  local copies, waits for them, and re-layouts  62.3 us (10%)
  between operations  15.5 us (2%)
    unnamed x8, waiting for transfers between devices  252 us
    reduce_scatter x1, waiting for transfers between devices, local(): lax.psum_scatter(down_grad.astype(jnp.bfloat16), 'dp', scatter_dimension=...  80.3 us
    all_gather x1, waiting for transfers between devices, local(): full_cot = lax.all_gather(cotangent, 'mp', axis=1, tiled=True)  69.3 us
    all_gather x1, waiting for transfers between devices, local(): full_tokens = lax.all_gather(tokens, 'mp', axis=1, tiled=True)  63.8 us
    unnamed x18, local copies, waits for them, and re-layouts  26.8 us
    reduce_scatter x1, waiting for transfers between devices, local(): lax.psum_scatter(up_grad.astype(jnp.bfloat16), 'dp', scatter_dimension=1,...  14.8 us
    dot_general x1, matrix products, local(): jnp.einsum('tsn,sd->tdn', down_terms, pick_table(down_columns, DB), preci...  13.1 us
    dot_general x1, matrix products, local(): jnp.einsum('tsk,sd->tdk', input_terms, pick_table(up_rows, DB), precision...  13 us
  transfers between devices with their start and end apart: 6, of which 6 were waited for; matrix products, arithmetic and copies ran while one was open for 12% of the time, Pallas kernels for 0%

commit v1 on v0

v1 whole, which is shorter than its diff:
```python
import functools
import math

import jax
import jax.numpy as jnp
from jax import lax
from jax.experimental import pallas as pl
from jax.experimental.pallas import tpu as pltpu
from jax.sharding import PartitionSpec as P

BLK = 256
HALF = 128
SLOTS = 12
ROWS = 768
MY_ROWS = 384
GROUPS = 3
PER = SLOTS // GROUPS
SLICE = 32
MESH = pl.DeviceIdType.MESH
BF = jnp.bfloat16
F32 = jnp.float32


def pack_pattern(rows, hidden, place, count):
    slot = jnp.arange(SLOTS, dtype=jnp.int32)
    local_hidden = hidden - place * 2
    pair = jnp.where(slot < count, local_hidden * 16 + rows, -1)
    match = pair[None, :] == jnp.arange(32, dtype=jnp.int32)[:, None]
    table = jnp.sum(jnp.where(match, slot[None, :] + 1, 0), axis=1)
    return table, local_hidden


def kernel(
    tok_in, cot_in, up_in, dn_in, meta_in,
    mixed_out, tg_out, ug_out, dg_out,
    acts_in, up_own, dn_own, up_other, dn_other, meta_v, meta_s, pre, bh, act, slope,
    pbuf, sbuf, rbuf, frecv,
    gd, gdr, gds, gdr2, gu, gur, gus, gur2,
    local_sem, swap_s, swap_r, z_s, z_r, sib_s, sib_r, w_s, w_r,
    rsib_s, rsib_r, ring_s, ring_r, fin_s, fin_r, g_s, g_r,
):
    d = lax.axis_index("dp")
    m = lax.axis_index("mp")
    y = lax.rem(d, 4)
    x_hi = d // 4
    z = m // 4
    x = lax.rem(m // 2, 2)
    c = lax.rem(m, 2)
    other_x = 1 - x
    other_c = 1 - c

    def place(hi, yy, zz, lo, cc):
        return (hi * 4 + yy, zz * 4 + lo * 2 + cc)

    z_next = place(x_hi, y, lax.rem(z + 1, 8), x, c)
    z_prev = place(x_hi, y, lax.rem(z + 7, 8), x, c)
    sibling = place(x_hi, y, z, x, other_c)
    partner = place(x_hi, y, z, other_x, c)
    flip_hi = 1 - x_hi
    x_up = place(lax.rem(x_hi + x, 2), y, z, other_x, c)
    x_down = place(lax.rem(x_hi + other_x, 2), y, z, other_x, c)
    x_peers = [partner, place(flip_hi, y, z, x, c), place(flip_hi, y, z, other_x, c)]
    peer_hi = [x_hi, flip_hi, flip_hi]
    peer_p = [1, 0, 1]
    y_peers = [place(x_hi, lax.rem(y + j, 4), z, x, c) for j in (1, 2, 3)]

    started = []

    def send(src, dst, s, r, dev):
        copy = pltpu.make_async_remote_copy(
            src_ref=src, dst_ref=dst, send_sem=s, recv_sem=r, device_id=dev, device_id_type=MESH
        )
        copy.start()
        started.append(copy)

    def arrived(ref, s, r):
        pltpu.make_async_remote_copy(
            src_ref=ref, dst_ref=ref, send_sem=s, recv_sem=r, device_id=sibling, device_id_type=MESH
        ).wait_recv()

    my_rows = pl.ds(pl.multiple_of(x * MY_ROWS, MY_ROWS), MY_ROWS)
    their_rows = pl.ds(pl.multiple_of(other_x * MY_ROWS, MY_ROWS), MY_ROWS)
    ins = [tok_in, cot_in]
    tiles = [[up_own, up_other], [dn_own, dn_other]]
    locals_ = []
    for a in range(2):
        locals_.append(
            pltpu.make_async_copy(ins[a].at[my_rows], acts_in.at[a, 0, c, x], local_sem.at[a])
        )
    for k, ref in enumerate((up_in, dn_in)):
        locals_.append(
            pltpu.make_async_copy(ref, tiles[k][0], local_sem.at[2 + k])
        )
    locals_.append(pltpu.make_async_copy(meta_in, meta_s.at[0], local_sem.at[4]))
    for copy in locals_:
        copy.start()

    barrier = pltpu.get_barrier_semaphore()
    peers = [z_next, z_prev, sibling] + x_peers + y_peers
    for dev in peers:
        pl.semaphore_signal(barrier, inc=1, device_id=dev, device_id_type=MESH)
    pl.semaphore_wait(barrier, len(peers))

    for a in range(2):
        send(ins[a].at[their_rows], acts_in.at[a, 0, c, x], swap_s.at[a], swap_r.at[a], partner)
    send(meta_in, meta_v, swap_s.at[2], swap_r.at[2], partner)

    def z_send(a, direction, index, src, dst):
        send(src, dst, z_s.at[a, direction, index], z_r.at[a, direction, index],
             z_prev if direction else z_next)

    def z_wait(a, direction, index, ref):
        arrived(ref, z_s.at[a, direction, index], z_r.at[a, direction, index])

    def sib_send(a, r):
        ref = acts_in.at[a, r, c]
        send(ref, ref, sib_s.at[a, r], sib_r.at[a, r], sibling)

    def sib_wait(a, r):
        arrived(acts_in.at[a, r, other_c], sib_s.at[a, r], sib_r.at[a, r])

    for a in range(2):
        locals_[a].wait()
        for direction, r in ((0, 1), (1, 7)):
            z_send(a, direction, 0, acts_in.at[a, 0, c, x], acts_in.at[a, r, c, x])
    for k in range(2):
        locals_[2 + k].wait()
        for half, dev in ((0, x_up), (1, x_down)):
            send(
                tiles[k][0].at[pl.ds(half * 6, 6)], tiles[k][1].at[pl.ds(half * 6, 6)],
                w_s.at[k, half], w_r.at[k, half], dev,
            )
    for a in range(2):
        arrived(acts_in.at[a, 0, c, other_x], swap_s.at[a], swap_r.at[a])
        for direction, r in ((0, 1), (1, 7)):
            z_send(a, direction, 1, acts_in.at[a, 0, c, other_x], acts_in.at[a, r, c, other_x])
        sib_send(a, 0)
    locals_[4].wait()
    arrived(meta_v, swap_s.at[2], swap_r.at[2])
    to_smem = pltpu.make_async_copy(meta_v, meta_s.at[1], local_sem.at[5])
    to_smem.start()

    def tile(kind, p, h, b):
        found = meta_s[p, kind, h * 16 + b]
        value = tiles[kind][p][jnp.maximum(found - 1, 0)]
        return jnp.where(found > 0, value, jnp.zeros_like(value))

    sums = [pre, bh]

    def accumulate(a, p, r, first):
        left = jnp.concatenate(
            [acts_in[a, r, 0, 0], acts_in[a, r, 1, 0], acts_in[a, r, 0, 1], acts_in[a, r, 1, 1]], axis=1
        )
        b = 2 * lax.rem(z + 8 - r, 8)
        for h in range(2):
            w0, w1 = tile(a, p, h, b), tile(a, p, h, b + 1)
            if a == 0:
                out = jnp.dot(left, jnp.concatenate([w0, w1], axis=0), preferred_element_type=F32)
            else:
                out = lax.dot_general(
                    left, jnp.concatenate([w0, w1], axis=1), (((1,), (1,)), ((), ())),
                    preferred_element_type=F32,
                )
            if first:
                sums[a][p * 2 + h] = out
            else:
                sums[a][p * 2 + h] += out

    for k in (1, 2, 3):
        for a in range(2):
            for direction, r in ((0, k), (1, 8 - k)):
                if k == 1:
                    z_wait(a, direction, 0, acts_in.at[a, r, c, x])
                    z_wait(a, direction, 1, acts_in.at[a, r, c, other_x])
                else:
                    z_wait(a, direction, k, acts_in.at[a, r, c])
                if k < 3:
                    z_send(a, direction, k + 1, acts_in.at[a, r, c],
                           acts_in.at[a, r + 1 - 2 * direction, c])
                else:
                    z_send(a, direction, 4, acts_in.at[a, r, c, direction],
                           acts_in.at[a, 4, c, direction])
                sib_send(a, r)
        for a in range(2):
            for r in ((0,) if k == 1 else (k - 1, 9 - k)):
                sib_wait(a, r)
                accumulate(a, 0, r, k == 1)
    for a in range(2):
        for direction in range(2):
            z_wait(a, direction, 4, acts_in.at[a, 4, c, direction])
        sib_send(a, 4)
    to_smem.wait()
    for a in range(2):
        for half in range(2):
            arrived(tiles[a][1].at[pl.ds(half * 6, 6)], w_s.at[a, half], w_r.at[a, half])
        for r in (3, 5, 4):
            sib_wait(a, r)
            accumulate(a, 0, r, False)
        accumulate(a, 1, 0, True)

        def rest(r, carry, a=a):
            accumulate(a, 1, r, False)
            return carry

        lax.fori_loop(1, 8, rest, 0)
        if a == 0:

            def gelu_step(i, carry):
                h = i // 6
                rows = pl.ds(pl.multiple_of(lax.rem(i, 6) * 64, 64), 64)
                v = pre[h, rows]
                cdf = 0.5 * (1.0 + lax.erf(v * 0.7071067811865476))
                act[h, rows] = (v * cdf).astype(BF)
                pre[h, rows] = cdf + v * jnp.exp(-0.5 * v * v) * 0.3989422804014327
                return carry

            lax.fori_loop(0, 24, gelu_step, 0)

    def slope_step(i, carry):
        h = i // 6
        rows = pl.ds(pl.multiple_of(lax.rem(i, 6) * 64, 64), 64)
        slope[h, rows] = (bh[h, rows] * pre[h, rows]).astype(BF)
        return carry

    lax.fori_loop(0, 24, slope_step, 0)

    lefts = [act, slope]

    def partial(o, q):
        left = jnp.concatenate([lefts[o][h] for h in range(4)], axis=1)
        b = 2 * lax.rem(z + q, 8)
        kind = 1 - o
        for xx in range(2):
            ws = [tile(kind, h // 2, h % 2, b + xx) for h in range(4)]
            if o == 0:
                out = jnp.dot(left, jnp.concatenate(ws, axis=0), preferred_element_type=F32)
            else:
                out = lax.dot_general(
                    left, jnp.concatenate(ws, axis=1), (((1,), (1,)), ((), ())),
                    preferred_element_type=F32,
                )
            out = out.astype(BF)
            for half in range(2):
                pbuf[o, q, half, xx] = out[:, half * HALF:(half + 1) * HALF]
        send(pbuf.at[o, q, other_c], sbuf.at[o, q], rsib_s.at[o, q], rsib_r.at[o, q], sibling)

    def add_sibling(o, q, extra):
        arrived(sbuf.at[o, q], rsib_s.at[o, q], rsib_r.at[o, q])
        for xx in range(2):
            total = pbuf[o, q, c, xx].astype(F32) + sbuf[o, q, xx].astype(F32)
            for more in extra[xx]:
                total += more().astype(F32)
            pbuf[o, q, c, xx] = total.astype(BF)

    def ring_send(o, direction, step, src, dst):
        send(src, dst, ring_s.at[o, direction, step], ring_r.at[o, direction, step],
             z_prev if direction else z_next)

    def ring_wait(o, direction, step, ref):
        arrived(ref, ring_s.at[o, direction, step], ring_r.at[o, direction, step])

    scale = 1.0 / math.sqrt(ROWS * 8)

    def grad_product(kind, p, i):
        if kind == 0:
            block, h = meta_s[p, 2, i], meta_s[p, 3, i]
        else:
            block, h = meta_s[p, 5, i], meta_s[p, 4, i]
        r = lax.rem(z + 8 - block // 2, 8)
        xx = lax.rem(block, 2)
        wide = jnp.concatenate([acts_in[kind, r, 0, xx], acts_in[kind, r, 1, xx]], axis=1)
        hidden = lefts[1 - kind][p * 2 + h]
        a, b = (wide, hidden) if kind == 0 else (hidden, wide)
        out = lax.dot_general(a, b, (((0,), (0,)), ((), ())), preferred_element_type=F32)
        live = jnp.where(i < meta_s[p, 6, kind], scale, 0.0)
        return (out * live).astype(BF)

    def down_group(g):
        def one(t, carry):
            p, i = t // PER, lax.rem(t, PER)
            out = grad_product(1, p, g * PER + i)
            for part in range(8):
                gd[g, part % 4, part // 4, p, i] = out[part * SLICE:(part + 1) * SLICE]
            return carry

        lax.fori_loop(0, 2 * PER, one, 0)
        for j in range(3):
            send(gd.at[g, lax.rem(y + j + 1, 4)], gdr.at[g, j],
                 g_s.at[0, g, j], g_r.at[0, g, j], y_peers[j])

    def up_group(g):
        def one(t, carry):
            p, i = t // PER, lax.rem(t, PER)
            out = grad_product(0, p, g * PER + i)
            for part in range(8):
                gu[g, part // 4, p, part % 4, i] = out[part * SLICE:(part + 1) * SLICE]
            return carry

        lax.fori_loop(0, 2 * PER, one, 0)
        for j in range(3):
            send(gu.at[g, peer_hi[j], peer_p[j]], gur.at[g, j],
                 g_s.at[1, g, j], g_r.at[1, g, j], x_peers[j])

    def down_second(g):
        for j in range(3):
            arrived(gdr.at[g, j], g_s.at[0, g, j], g_r.at[0, g, j])
        for hi in range(2):
            for p in range(2):
                total = gd[g, y, hi, p].astype(F32)
                for j in range(3):
                    total += gdr[g, j, hi, p].astype(F32)
                gds[g, hi, p] = total.astype(BF)
        for j in range(3):
            send(gds.at[g, peer_hi[j], peer_p[j]], gdr2.at[g, j],
                 g_s.at[2, g, j], g_r.at[2, g, j], x_peers[j])

    def up_second(g):
        for j in range(3):
            arrived(gur.at[g, j], g_s.at[1, g, j], g_r.at[1, g, j])
        for yy in range(4):
            total = gu[g, x_hi, 0, yy].astype(F32)
            for j in range(3):
                total += gur[g, j, yy].astype(F32)
            gus[g, yy] = total.astype(BF)
        for j in range(3):
            send(gus.at[g, lax.rem(y + j + 1, 4)], gur2.at[g, j],
                 g_s.at[3, g, j], g_r.at[3, g, j], y_peers[j])

    def down_last(g):
        for j in range(3):
            arrived(gdr2.at[g, j], g_s.at[2, g, j], g_r.at[2, g, j])
        total = gds[g, x_hi, 0].astype(F32)
        for j in range(3):
            total += gdr2[g, j].astype(F32)
        dg_out[g * PER:(g + 1) * PER] = total

    def up_last(g):
        for j in range(3):
            arrived(gur2.at[g, j], g_s.at[3, g, j], g_r.at[3, g, j])
        total = gus[g, y].astype(F32)
        for j in range(3):
            total += gur2[g, j].astype(F32)
        ug_out[g * PER:(g + 1) * PER] = total

    for o in range(2):
        partial(o, 4)
    down_group(0)
    up_group(0)
    for o in range(2):
        add_sibling(o, 4, [[], []])
        for direction in range(2):
            ring_send(o, direction, 0, pbuf.at[o, 4, c, direction], rbuf.at[o, direction, 0, direction])
        partial(o, 3)
        partial(o, 5)
    down_group(1)
    up_group(1)
    for step in (1, 2, 3):
        for o in range(2):
            for direction in range(2):
                q = 4 + step if direction else 4 - step
                came = rbuf.at[o, direction, step - 1]
                if step == 1:
                    ring_wait(o, direction, 0, came.at[direction])
                    extra = [[], []]
                    extra[direction] = [lambda came=came, xx=direction: came[xx]]
                else:
                    ring_wait(o, direction, step - 1, came)
                    extra = [[lambda came=came, xx=xx: came[xx]] for xx in range(2)]
                add_sibling(o, q, extra)
                ring_send(o, direction, step, pbuf.at[o, q, c], rbuf.at[o, direction, step])
            if step < 3:
                partial(o, 3 - step)
                partial(o, 5 + step)
            else:
                partial(o, 0)
        if step == 1:
            down_group(2)
            up_group(2)
    for g in range(GROUPS):
        down_second(g)
        up_second(g)
    outs = [mixed_out, tg_out]
    for o in range(2):
        for direction in range(2):
            ring_wait(o, direction, 3, rbuf.at[o, direction, 3])
        add_sibling(
            o, 0,
            [[lambda xx=xx, e=e: rbuf[o, e, 3, xx] for e in range(2)] for xx in range(2)],
        )
        send(pbuf.at[o, 0, c, other_x], frecv.at[o], fin_s.at[o], fin_r.at[o], partner)
        outs[o][my_rows] = pbuf[o, 0, c, x]
    for g in range(GROUPS):
        down_last(g)
        up_last(g)
    for o in range(2):
        arrived(frecv.at[o], fin_s.at[o], fin_r.at[o])
        outs[o][their_rows] = frecv[o]
    for copy in started:
        copy.wait_send()


def local(
    tokens, cotangent, up_tiles, up_rows, up_columns, up_counts,
    down_tiles, down_rows, down_columns, down_counts,
):
    place = lax.axis_index("mp")
    up_table, up_hidden = pack_pattern(up_rows, up_columns, place, up_counts[0])
    down_table, down_hidden = pack_pattern(down_columns, down_rows, place, down_counts[0])
    counts = jnp.concatenate([up_counts, down_counts])
    meta = jnp.stack(
        [
            jnp.pad(v, (0, 128 - v.shape[0]))
            for v in (up_table, down_table, up_rows, up_hidden, down_hidden, down_columns, counts, counts)
        ]
    )
    dma = pltpu.SemaphoreType.DMA
    vm = pltpu.VMEM
    any_space = pl.BlockSpec(memory_space=pl.ANY)
    in_vmem = pl.BlockSpec(memory_space=pltpu.VMEM)
    return tuple(
        pl.pallas_call(
            kernel,
            out_shape=(
                jax.ShapeDtypeStruct((ROWS, HALF), BF),
                jax.ShapeDtypeStruct((ROWS, HALF), BF),
                jax.ShapeDtypeStruct((SLOTS, SLICE, BLK), F32),
                jax.ShapeDtypeStruct((SLOTS, SLICE, BLK), F32),
            ),
            in_specs=[any_space] * 4 + [in_vmem],
            out_specs=(in_vmem,) * 4,
            scratch_shapes=[
                vm((2, 8, 2, 2, MY_ROWS, HALF), BF),
                vm((SLOTS, BLK, BLK), BF), vm((SLOTS, BLK, BLK), BF),
                vm((SLOTS, BLK, BLK), BF), vm((SLOTS, BLK, BLK), BF),
                vm((8, 128), jnp.int32),
                pltpu.SMEM((2, 8, 128), jnp.int32),
                vm((4, MY_ROWS, BLK), F32),
                vm((4, MY_ROWS, BLK), F32),
                vm((4, MY_ROWS, BLK), BF),
                vm((4, MY_ROWS, BLK), BF),
                vm((2, 8, 2, 2, MY_ROWS, HALF), BF),
                vm((2, 8, 2, MY_ROWS, HALF), BF),
                vm((2, 2, 4, 2, MY_ROWS, HALF), BF),
                vm((2, MY_ROWS, HALF), BF),
                vm((GROUPS, 4, 2, 2, PER, SLICE, BLK), BF),
                vm((GROUPS, 3, 2, 2, PER, SLICE, BLK), BF),
                vm((GROUPS, 2, 2, PER, SLICE, BLK), BF),
                vm((GROUPS, 3, PER, SLICE, BLK), BF),
                vm((GROUPS, 2, 2, 4, PER, SLICE, BLK), BF),
                vm((GROUPS, 3, 4, PER, SLICE, BLK), BF),
                vm((GROUPS, 4, PER, SLICE, BLK), BF),
                vm((GROUPS, 3, PER, SLICE, BLK), BF),
                dma((6,)),
                dma((3,)), dma((3,)),
                dma((2, 2, 5)), dma((2, 2, 5)),
                dma((2, 8)), dma((2, 8)),
                dma((2, 2)), dma((2, 2)),
                dma((2, 8)), dma((2, 8)),
                dma((2, 2, 4)), dma((2, 2, 4)),
                dma((2,)), dma((2,)),
                dma((4, GROUPS, 3)), dma((4, GROUPS, 3)),
            ],
            compiler_params=pltpu.CompilerParams(
                collective_id=0, has_side_effects=True, vmem_limit_bytes=58 << 20
            ),
            name="sparse_feed_forward",
        )(tokens, cotangent, up_tiles, down_tiles, meta)
    )


def solution(mesh):
    return jax.shard_map(
        local,
        mesh=mesh,
        in_specs=(
            P("dp", "mp"),
            P("dp", "mp"),
            P("mp", None, None),
            P("mp"),
            P("mp"),
            P("mp"),
            P("mp", None, None),
            P("mp"),
            P("mp"),
            P("mp"),
        ),
        out_specs=(P("dp", "mp"), P("dp", "mp"), P("mp", "dp", None), P("mp", "dp", None)),
        check_vma=False,
    )
```

time: 640 us -> 118 us (0.18)
  waiting for transfers between devices: 481 us -> 0 us
  Pallas kernels: 0 us -> 107 us
  matrix products: 73.8 us -> 0 us
  local copies, waits for them, and re-layouts: 62.3 us -> 7.75 us
  between operations: 15.5 us -> 1.97 us
    unnamed x8 -> x0, waiting for transfers between devices: 252 us -> none
    all_gather x2 -> x0, waiting for transfers between devices: 133 us -> none  [the longest x1 69.3 us: local(): full_cot = lax.all_gather(cotangent, 'mp', axis=1, tiled=True)]
    pallas_call x0 -> x1, Pallas kernels: none -> 107 us  [local(): pl.pallas_call(kernel, out_shape=(jax.ShapeDtypeStruct((ROWS, HALF), BF),...]
    reduce_scatter x2 -> x0, waiting for transfers between devices: 95.1 us -> none  [the longest x1 80.3 us: local(): lax.psum_scatter(down_grad.astype(jnp.bfloat16), 'dp', scatter_dimension=...]
    dot_general x10 -> x0, matrix products: 73.8 us -> none  [the longest x1 13.1 us: local(): jnp.einsum('tsn,sd->tdn', down_terms, pick_table(down_columns, DB), preci...]
    unnamed x18 -> x6, local copies, waits for them, and re-layouts: 26.8 us -> 5.8 us
    gather x4 -> x0, local copies, waits for them, and re-layouts: 18.3 us -> none  [the longest x1 6.02 us: local(): cot_gathered = full_cot.reshape(tok_rows, DB, BLK)[:, down_columns]]
    reshape x2 -> x0, local copies, waits for them, and re-layouts: 17.2 us -> none  [the longest x1 8.66 us: local(): cot_gathered = full_cot.reshape(tok_rows, DB, BLK)[:, down_columns]]
  transfers between devices with their start and end apart: 6 -> 0, of which waited for: 6 -> 0; matrix products, arithmetic and copies ran while one was open for 12% -> 0% of each run, Pallas kernels for 0% -> 0%
where the time goes in v1:
time: 118 us
  Pallas kernels  107 us (91%)
  local copies, waits for them, and re-layouts  7.75 us (7%)
  between operations  1.97 us (2%)
    pallas_call x1, Pallas kernels, local(): pl.pallas_call(kernel, out_shape=(jax.ShapeDtypeStruct((ROWS, HALF), BF),...  107 us
    unnamed x6, local copies, waits for them, and re-layouts  5.8 us

profile of v1, /device:TPU:8, one launch (start us, length us, event | category | flops | bytes accessed | tf_op | source)
XLA Modules:
  0.0 117.7 jit_solution(1650013260073231230)
XLA Ops:
  1.9 0.7 pad_bitcast_fusion.4
  2.6 0.1 pad_add_fusion
  2.7 0.7 pad_bitcast_fusion
  3.3 0.7 compare_select_fusion
  4.0 0.1 select_reduce_fusion
  4.2 0.6 stack.32.meta_in
  4.8 107.1 %sparse_feed_forward.1 = (bf16[768,128]{1,0:T(8,128)(2,1)}, bf16[768,128]{1,0:T(8,128)(2,1)}, f32[12,32,256]{2,1,0:T(8,128)}, f32[12,32,256]{2,1,0:T(8,128)}) custom-call(bf16[768,128]{1,0:T(8,128)(2,1)} %tok_in.1, bf16[768,128]{1,0:T(8,128)(2,1)} %cot_in.1, bf16[12,256,256]{2,1,0:T(8,128)(2,1)} %up_in.1, bf16[12,256,256]{2,1,0:T(8,128)(2,1)} %dn_in.1, ...), custom_call_target="tpu_custom_call" | custom-call | tf_op jit(solution)/shard_map/sparse_feed_forward/pallas_call | solution.py:421
  111.9 0.0 copy-start
  111.9 1.7 %copy.20 = bf16[768,128]{1,0:T(8,128)(2,1)} copy(bf16[768,128]{1,0:T(8,128)(2,1)} %get-tuple-element.18) | data formatting | bytes 393216
  113.6 1.6 %copy.21 = bf16[768,128]{1,0:T(8,128)(2,1)} copy(bf16[768,128]{1,0:T(8,128)(2,1)} %get-tuple-element.19) | data formatting | bytes 393216
  115.2 1.8 %copy.22 = f32[12,32,256]{2,1,0:T(8,128)} copy(f32[12,32,256]{2,1,0:T(8,128)} %get-tuple-element.20) | data formatting | bytes 786432
  117.0 0.0 copy-done
  117.0 0.7 copy.23
  (5 shorter events, 0.0 us)
Async XLA Ops:
  111.9 5.1 %copy-start = (f32[12,32,256]{2,1,0:T(8,128)S(1)}, f32[12,32,256]{2,1,0:T(8,128)}, u32[]{:S(2)}) copy-start(f32[12,32,256]{2,1,0:T(8,128)} %get-tuple-element.21) | copy-start | bytes 1179652

commit v2 on v1

v2 whole, which is shorter than its diff:
```python
import functools
import math

import jax
import jax.numpy as jnp
from jax import lax
from jax.experimental import pallas as pl
from jax.experimental.pallas import tpu as pltpu
from jax.sharding import PartitionSpec as P

BLK = 256
HALF = 128
SLOTS = 12
ROWS = 768
MY_ROWS = 384
GROUPS = 3
PER = SLOTS // GROUPS
SLICE = 32
MESH = pl.DeviceIdType.MESH
BF = jnp.bfloat16
F32 = jnp.float32


def pack_pattern(up_rows, up_columns, up_counts, down_rows, down_columns, down_counts):
    lane = lax.broadcasted_iota(jnp.int32, (8, 128), 1)
    row = lax.broadcasted_iota(jnp.int32, (8, 128), 0)
    ups, downs = up_counts[0], down_counts[0]
    packed = jnp.where((row == 6) & (lane == 0), ups, 0)
    packed = jnp.where((row == 6) & (lane == 1), downs, packed)
    for s in range(SLOTS):
        up_row, up_hidden = up_rows[s], up_columns[s] & 1
        down_hidden, down_column = down_rows[s] & 1, down_columns[s]
        up_pair = jnp.where(s < ups, up_hidden * 16 + up_row, -1)
        down_pair = jnp.where(s < downs, down_hidden * 16 + down_column, -1)
        found = ((row == 0) & (lane == up_pair)) | ((row == 1) & (lane == down_pair))
        packed = jnp.where(found, s + 1, packed)
        for at, value in ((2, up_row), (3, up_hidden), (4, down_hidden), (5, down_column)):
            packed = jnp.where((row == at) & (lane == s), value, packed)
    return packed


def kernel(
    tok_in, cot_in, up_in, dn_in, up_rows, up_columns, up_counts, down_rows, down_columns, down_counts,
    mixed_out, tg_out, ug_out, dg_out,
    acts_in, up_own, dn_own, up_other, dn_other, meta_own, meta_v, meta_s, pre, bh, act, slope, tok_t, act_t,
    pbuf, sbuf, rbuf, frecv,
    gd, gda, gdr, gds, gdr2, gu, gua, gur, gus, gur2,
    local_sem, swap_s, swap_r, z_s, z_r, sib_s, sib_r, w_s, w_r,
    rsib_s, rsib_r, ring_s, ring_r, fin_s, fin_r, g_s, g_r,
):
    d = lax.axis_index("dp")
    m = lax.axis_index("mp")
    y = lax.rem(d, 4)
    x_hi = d // 4
    z = m // 4
    x = lax.rem(m // 2, 2)
    c = lax.rem(m, 2)
    other_x = 1 - x
    other_c = 1 - c

    def place(hi, yy, zz, lo, cc):
        return (hi * 4 + yy, zz * 4 + lo * 2 + cc)

    z_next = place(x_hi, y, lax.rem(z + 1, 8), x, c)
    z_prev = place(x_hi, y, lax.rem(z + 7, 8), x, c)
    sibling = place(x_hi, y, z, x, other_c)
    partner = place(x_hi, y, z, other_x, c)
    flip_hi = 1 - x_hi
    x_up = place(lax.rem(x_hi + x, 2), y, z, other_x, c)
    x_down = place(lax.rem(x_hi + other_x, 2), y, z, other_x, c)
    x_peers = [partner, place(flip_hi, y, z, x, c), place(flip_hi, y, z, other_x, c)]
    peer_hi = [x_hi, flip_hi, flip_hi]
    peer_p = [1, 0, 1]
    y_peers = [place(x_hi, lax.rem(y + j, 4), z, x, c) for j in (1, 2, 3)]

    barrier = pltpu.get_barrier_semaphore()
    peers = [z_next, z_prev, sibling] + x_peers + y_peers
    for dev in peers:
        pl.semaphore_signal(barrier, inc=1, device_id=dev, device_id_type=MESH)

    started = []

    def send(src, dst, s, r, dev):
        copy = pltpu.make_async_remote_copy(
            src_ref=src, dst_ref=dst, send_sem=s, recv_sem=r, device_id=dev, device_id_type=MESH
        )
        copy.start()
        started.append(copy)

    def arrived(ref, s, r):
        pltpu.make_async_remote_copy(
            src_ref=ref, dst_ref=ref, send_sem=s, recv_sem=r, device_id=sibling, device_id_type=MESH
        ).wait_recv()

    my_rows = pl.ds(pl.multiple_of(x * MY_ROWS, MY_ROWS), MY_ROWS)
    their_rows = pl.ds(pl.multiple_of(other_x * MY_ROWS, MY_ROWS), MY_ROWS)
    ins = [tok_in, cot_in]
    tiles = [[up_own, up_other], [dn_own, dn_other]]
    locals_ = []
    for a in range(2):
        locals_.append(
            pltpu.make_async_copy(ins[a].at[my_rows], acts_in.at[a, 0, c, x], local_sem.at[a])
        )
    for k, ref in enumerate((up_in, dn_in)):
        locals_.append(
            pltpu.make_async_copy(ref, tiles[k][0], local_sem.at[2 + k])
        )
    for copy in locals_:
        copy.start()
    meta_own[...] = pack_pattern(up_rows, up_columns, up_counts, down_rows, down_columns, down_counts)
    locals_.append(pltpu.make_async_copy(meta_own, meta_s.at[0], local_sem.at[4]))
    locals_[4].start()

    pl.semaphore_wait(barrier, len(peers))

    for a in range(2):
        send(ins[a].at[their_rows], acts_in.at[a, 0, c, x], swap_s.at[a], swap_r.at[a], partner)
    send(meta_own, meta_v, swap_s.at[2], swap_r.at[2], partner)

    def z_send(a, direction, step, block, src, dst):
        send(src, dst, z_s.at[a, direction, step, block], z_r.at[a, direction, step, block],
             z_prev if direction else z_next)

    def z_wait(a, direction, step, block, ref):
        arrived(ref, z_s.at[a, direction, step, block], z_r.at[a, direction, step, block])

    def sib_send(a, r):
        ref = acts_in.at[a, r, c]
        send(ref, ref, sib_s.at[a, r], sib_r.at[a, r], sibling)

    def sib_wait(a, r):
        arrived(acts_in.at[a, r, other_c], sib_s.at[a, r], sib_r.at[a, r])

    def quarter(i):
        return pl.ds(3 * lax.rem(y + i, 4), 3)

    def send_own(a):
        locals_[a].wait()
        for direction, r in ((0, 1), (1, 7)):
            z_send(a, direction, 0, x, acts_in.at[a, 0, c, x], acts_in.at[a, r, c, x])

    def swap_done(a):
        arrived(acts_in.at[a, 0, c, other_x], swap_s.at[a], swap_r.at[a])
        sib_send(a, 0)

    def send_swapped(a):
        for direction, r in ((0, 1), (1, 7)):
            z_send(a, direction, 0, other_x, acts_in.at[a, 0, c, other_x], acts_in.at[a, r, c, other_x])

    send_own(0)
    for k in range(2):
        locals_[2 + k].wait()
        for i, dev in ((0, x_up), (1, x_down)):
            send(tiles[k][0].at[quarter(i)], tiles[k][1].at[quarter(i)], w_s.at[k, i], w_r.at[k, i], dev)
    swap_done(0)
    send_swapped(0)
    send_own(1)
    locals_[4].wait()
    arrived(meta_v, swap_s.at[2], swap_r.at[2])
    to_smem = pltpu.make_async_copy(meta_v, meta_s.at[1], local_sem.at[5])
    to_smem.start()
    swap_done(1)

    def tile(kind, p, h, b):
        found = meta_s[p, kind, h * 16 + b]
        value = tiles[kind][p][jnp.maximum(found - 1, 0)]
        return jnp.where(found > 0, value, jnp.zeros_like(value))

    def pass_weights(k):
        for i, j, dev in ((0, 3, y_peers[0]), (1, 2, y_peers[2])):
            ref = tiles[k][1].at[quarter(i)]
            arrived(ref, w_s.at[k, i], w_r.at[k, i])
            send(ref, ref, w_s.at[k, j], w_r.at[k, j], dev)

    def rest_of_weights(k):
        for j in (2, 3):
            arrived(tiles[k][1].at[quarter(j)], w_s.at[k, j], w_r.at[k, j])

    sums = [pre, bh]

    def accumulate(a, p, r, first):
        left = jnp.concatenate(
            [acts_in[a, r, 0, 0], acts_in[a, r, 1, 0], acts_in[a, r, 0, 1], acts_in[a, r, 1, 1]], axis=1
        )
        if a == 0 and p == 0:
            for xx in range(2):
                tok_t[r, xx] = left[:, xx * BLK:(xx + 1) * BLK].T
        b = 2 * lax.rem(z + 8 - r, 8)
        for h in range(2):
            w0, w1 = tile(a, p, h, b), tile(a, p, h, b + 1)
            if a == 0:
                out = jnp.dot(left, jnp.concatenate([w0, w1], axis=0), preferred_element_type=F32)
            else:
                out = lax.dot_general(
                    left, jnp.concatenate([w0, w1], axis=1), (((1,), (1,)), ((), ())),
                    preferred_element_type=F32,
                )
            if first:
                sums[a][p * 2 + h] = out
            else:
                sums[a][p * 2 + h] += out

    def forward(a, k):
        for block in (x, other_x):
            for direction, r in ((0, k), (1, 8 - k)):
                z_wait(a, direction, k - 1, block, acts_in.at[a, r, c, block])
                if k < 3:
                    z_send(a, direction, k, block, acts_in.at[a, r, c, block],
                           acts_in.at[a, r + 1 - 2 * direction, c, block])
        for direction, r in ((0, k), (1, 8 - k)):
            if k == 3:
                z_send(a, direction, 3, direction, acts_in.at[a, r, c, direction],
                       acts_in.at[a, 4, c, direction])
            sib_send(a, r)

    def last_unit(a):
        for direction in range(2):
            z_wait(a, direction, 3, direction, acts_in.at[a, 4, c, direction])
        sib_send(a, 4)

    def own_products(a, units):
        for r in units:
            sib_wait(a, r)
            accumulate(a, 0, r, r == 0)

    def other_products(a):
        accumulate(a, 1, 0, True)

        def rest(r, carry):
            accumulate(a, 1, r, False)
            return carry

        lax.fori_loop(1, 8, rest, 0)

    def gelu_step(i, carry):
        h = i // 6
        rows = pl.ds(pl.multiple_of(lax.rem(i, 6) * 64, 64), 64)
        v = pre[h, rows]
        cdf = 0.5 * (1.0 + lax.erf(v * 0.7071067811865476))
        act[h, rows] = (v * cdf).astype(BF)
        pre[h, rows] = cdf + v * jnp.exp(-0.5 * v * v) * 0.3989422804014327
        return carry

    def slope_step(i, carry):
        h = i // 6
        rows = pl.ds(pl.multiple_of(lax.rem(i, 6) * 64, 64), 64)
        slope[h, rows] = (bh[h, rows] * pre[h, rows]).astype(BF)
        return carry

    lefts = [act, slope]

    def partial(o, q):
        left = jnp.concatenate([lefts[o][h] for h in range(4)], axis=1)
        b = 2 * lax.rem(z + q, 8)
        kind = 1 - o
        for xx in range(2):
            ws = [tile(kind, h // 2, h % 2, b + xx) for h in range(4)]
            if o == 0:
                out = jnp.dot(left, jnp.concatenate(ws, axis=0), preferred_element_type=F32)
            else:
                out = lax.dot_general(
                    left, jnp.concatenate(ws, axis=1), (((1,), (1,)), ((), ())),
                    preferred_element_type=F32,
                )
            out = out.astype(BF)
            for half in range(2):
                pbuf[o, q, half, xx] = out[:, half * HALF:(half + 1) * HALF]
        send(pbuf.at[o, q, other_c], sbuf.at[o, q], rsib_s.at[o, q], rsib_r.at[o, q], sibling)

    def sibling_part(o, q):
        arrived(sbuf.at[o, q], rsib_s.at[o, q], rsib_r.at[o, q])

    def add(o, q, xx, came):
        total = pbuf[o, q, c, xx].astype(F32) + sbuf[o, q, xx].astype(F32)
        for ref in came:
            total += ref[...].astype(F32)
        pbuf[o, q, c, xx] = total.astype(BF)

    def ring_send(o, direction, step, xx):
        q = 4 + step if direction else 4 - step
        send(pbuf.at[o, q, c, xx], rbuf.at[o, direction, step, xx],
             ring_s.at[o, direction, step, xx], ring_r.at[o, direction, step, xx],
             z_prev if direction else z_next)

    def ring_wait(o, direction, step, xx):
        ref = rbuf.at[o, direction, step, xx]
        arrived(ref, ring_s.at[o, direction, step, xx], ring_r.at[o, direction, step, xx])
        return ref

    def ring_first(o):
        sibling_part(o, 4)
        for direction in range(2):
            add(o, 4, direction, [])
            ring_send(o, direction, 0, direction)

    def ring_step(o, step):
        for q in (4 - step, 4 + step):
            sibling_part(o, q)
        if step == 1:
            for direction in range(2):
                add(o, 4 + step if direction else 4 - step, 1 - direction, [])
                ring_send(o, direction, step, 1 - direction)
            for direction in range(2):
                came = ring_wait(o, direction, 0, direction)
                add(o, 4 + step if direction else 4 - step, direction, [came])
                ring_send(o, direction, step, direction)
            return
        for xx in (other_x, x):
            for direction in range(2):
                came = ring_wait(o, direction, step - 1, xx)
                add(o, 4 + step if direction else 4 - step, xx, [came])
                ring_send(o, direction, step, xx)

    outs = [mixed_out, tg_out]

    def ring_last(o):
        sibling_part(o, 0)
        for xx in (other_x, x):
            add(o, 0, xx, [ring_wait(o, direction, 3, xx) for direction in range(2)])
            if xx is other_x:
                send(pbuf.at[o, 0, c, other_x], frecv.at[o], fin_s.at[o], fin_r.at[o], partner)
        outs[o][my_rows] = pbuf[o, 0, c, x]

    def gelu():
        lax.fori_loop(0, 24, gelu_step, 0)

    def slopes():
        lax.fori_loop(0, 24, slope_step, 0)

    def turn():
        for h in range(4):
            act_t[h] = act[h].T

    def fin_last(o):
        arrived(frecv.at[o], fin_s.at[o], fin_r.at[o])
        outs[o][their_rows] = frecv[o]

    scale = 1.0 / math.sqrt(ROWS * 8)

    def grad_product(kind, p, i):
        if kind == 0:
            block, h = meta_s[p, 2, i], meta_s[p, 3, i]
        else:
            block, h = meta_s[p, 5, i], meta_s[p, 4, i]
        r = lax.rem(z + 8 - block // 2, 8)
        xx = lax.rem(block, 2)
        if kind == 0:
            left, right = tok_t[r, xx], slope[p * 2 + h]
        else:
            left = act_t[p * 2 + h]
            right = jnp.concatenate([acts_in[1, r, 0, xx], acts_in[1, r, 1, xx]], axis=1)
        out = jnp.dot(left, right, preferred_element_type=F32)
        live = jnp.where(i < meta_s[p, 6, kind], scale, 0.0)
        return (out * live).astype(BF)

    y_next, y_next2, y_prev = (lax.rem(y + j, 4) for j in (1, 2, 3))
    up_hi, down_hi = lax.rem(x_hi + x, 2), lax.rem(x_hi + other_x, 2)

    def grad_send(kind, g, i, src, dst, dev):
        send(src, dst, g_s.at[kind, g, i], g_r.at[kind, g, i], dev)

    def grad_wait(kind, g, i, ref):
        arrived(ref, g_s.at[kind, g, i], g_r.at[kind, g, i])

    def down_group(g):
        def one(t, carry):
            p, i = t // PER, lax.rem(t, PER)
            out = grad_product(1, p, g * PER + i)
            for part in range(8):
                gd[g, part % 4, part // 4, p, i] = out[part * SLICE:(part + 1) * SLICE]
            return carry

        lax.fori_loop(0, 2 * PER, one, 0)
        grad_send(0, g, 0, gd.at[g, y_next2, 0], gda.at[g, 0], y_peers[0])
        grad_send(0, g, 1, gd.at[g, y_next2, 1], gda.at[g, 1], y_peers[2])

    def down_mid(g):
        for i, to, hi, dev in ((0, y_next, 0, y_peers[0]), (1, y_prev, 1, y_peers[2])):
            grad_wait(0, g, i, gda.at[g, i])
            for p in range(2):
                gd[g, to, hi, p] = (gd[g, to, hi, p].astype(F32) + gda[g, i, p].astype(F32)).astype(BF)
            grad_send(0, g, 2 + i, gd.at[g, to], gdr.at[g, i], dev)

    def up_group(g):
        def one(t, carry):
            p, i = t // PER, lax.rem(t, PER)
            out = grad_product(0, p, g * PER + i)
            for part in range(8):
                gu[g, part // 4, p, part % 4, i] = out[part * SLICE:(part + 1) * SLICE]
            return carry

        lax.fori_loop(0, 2 * PER, one, 0)
        low, high = pl.ds(0, 2), pl.ds(2, 2)
        grad_send(1, g, 0, gu.at[g, flip_hi, 0, low], gua.at[g, 0], x_up)
        grad_send(1, g, 1, gu.at[g, flip_hi, 0, high], gua.at[g, 1], x_down)

    def up_mid(g):
        for i, hi, dev in ((0, up_hi, x_up), (1, down_hi, x_down)):
            grad_wait(1, g, i, gua.at[g, i])
            for yy in range(2):
                both = gu[g, hi, 1, 2 * i + yy].astype(F32) + gua[g, i, yy].astype(F32)
                gu[g, hi, 1, 2 * i + yy] = both.astype(BF)
            grad_send(1, g, 2 + i, gu.at[g, hi, 1], gur.at[g, i], dev)

    def down_second(g):
        for i in range(2):
            grad_wait(0, g, 2 + i, gdr.at[g, i])
        for hi in range(2):
            for p in range(2):
                total = gd[g, y, hi, p].astype(F32)
                for i in range(2):
                    total += gdr[g, i, hi, p].astype(F32)
                gds[g, hi, p] = total.astype(BF)
        for j in range(3):
            grad_send(2, g, j, gds.at[g, peer_hi[j], peer_p[j]], gdr2.at[g, j], x_peers[j])

    def up_second(g):
        for i in range(2):
            grad_wait(1, g, 2 + i, gur.at[g, i])
        for yy in range(4):
            total = gu[g, x_hi, 0, yy].astype(F32)
            for i in range(2):
                total += gur[g, i, yy].astype(F32)
            gus[g, yy] = total.astype(BF)
        for j in range(3):
            grad_send(3, g, j, gus.at[g, lax.rem(y + j + 1, 4)], gur2.at[g, j], y_peers[j])

    def down_last(g):
        for j in range(3):
            grad_wait(2, g, j, gdr2.at[g, j])
        total = gds[g, x_hi, 0].astype(F32)
        for j in range(3):
            total += gdr2[g, j].astype(F32)
        dg_out[g * PER:(g + 1) * PER] = total

    def up_last(g):
        for j in range(3):
            grad_wait(3, g, j, gur2.at[g, j])
        total = gus[g, y].astype(F32)
        for j in range(3):
            total += gur2[g, j].astype(F32)
        ug_out[g * PER:(g + 1) * PER] = total

    send_swapped(1)
    forward(0, 1)
    own_products(0, (0,))
    forward(1, 1)
    pass_weights(0)
    own_products(0, (1, 7))
    forward(0, 2)
    own_products(1, (0,))
    forward(1, 2)
    own_products(0, (2, 6))
    pass_weights(1)
    forward(0, 3)
    own_products(1, (1, 7))
    to_smem.wait()
    forward(1, 3)
    last_unit(0)
    own_products(0, (3, 5))
    rest_of_weights(0)
    own_products(0, (4,))
    other_products(0)
    gelu()
    turn()
    rest_of_weights(1)
    partial(0, 4)
    partial(0, 3)
    ring_first(0)
    own_products(1, (2, 6))
    partial(0, 5)
    accumulate(1, 1, 0, True)
    accumulate(1, 1, 1, False)
    accumulate(1, 1, 7, False)
    accumulate(1, 1, 2, False)
    accumulate(1, 1, 6, False)
    last_unit(1)
    own_products(1, (3, 5))
    accumulate(1, 1, 3, False)
    accumulate(1, 1, 5, False)
    sib_wait(1, 4)
    down_group(0)
    accumulate(1, 0, 4, False)
    accumulate(1, 1, 4, False)
    slopes()
    up_group(0)
    down_group(1)
    ring_step(0, 1)
    up_group(1)
    down_group(2)
    down_mid(0)
    up_mid(0)
    up_group(2)
    partial(1, 4)
    down_mid(1)
    up_mid(1)
    ring_first(1)
    partial(0, 2)
    partial(0, 6)
    down_mid(2)
    up_mid(2)
    ring_step(0, 2)
    partial(1, 3)
    partial(1, 5)
    ring_step(1, 1)
    down_second(0)
    up_second(0)
    partial(1, 2)
    partial(1, 6)
    partial(0, 1)
    partial(0, 7)
    ring_step(0, 3)
    down_second(1)
    up_second(1)
    ring_step(1, 2)
    partial(1, 1)
    partial(1, 7)
    partial(0, 0)
    down_second(2)
    up_second(2)
    ring_step(1, 3)
    partial(1, 0)
    ring_last(0)
    down_last(0)
    up_last(0)
    down_last(1)
    up_last(1)
    fin_last(0)
    ring_last(1)
    down_last(2)
    up_last(2)
    fin_last(1)
    for copy in started:
        copy.wait_send()


def hand_over(*refs):
    for i in range(4):
        refs[4 + i][...] = refs[i][...]


def local(
    tokens, cotangent, up_tiles, up_rows, up_columns, up_counts,
    down_tiles, down_rows, down_columns, down_counts,
):
    dma = pltpu.SemaphoreType.DMA
    vm = pltpu.VMEM
    any_space = pl.BlockSpec(memory_space=pl.ANY)
    in_vmem = pl.BlockSpec(memory_space=pltpu.VMEM)
    shapes = (
        jax.ShapeDtypeStruct((ROWS, HALF), BF),
        jax.ShapeDtypeStruct((ROWS, HALF), BF),
        jax.ShapeDtypeStruct((SLOTS, SLICE, BLK), F32),
        jax.ShapeDtypeStruct((SLOTS, SLICE, BLK), F32),
    )
    made = pl.pallas_call(
            kernel,
            out_shape=shapes,
            in_specs=[any_space] * 4 + [pl.BlockSpec(memory_space=pltpu.SMEM)] * 6,
            out_specs=(in_vmem,) * 4,
            scratch_shapes=[
                vm((2, 8, 2, 2, MY_ROWS, HALF), BF),
                vm((SLOTS, BLK, BLK), BF), vm((SLOTS, BLK, BLK), BF),
                vm((SLOTS, BLK, BLK), BF), vm((SLOTS, BLK, BLK), BF),
                vm((8, 128), jnp.int32), vm((8, 128), jnp.int32),
                pltpu.SMEM((2, 8, 128), jnp.int32),
                vm((4, MY_ROWS, BLK), F32),
                vm((4, MY_ROWS, BLK), F32),
                vm((4, MY_ROWS, BLK), BF),
                vm((4, MY_ROWS, BLK), BF),
                vm((8, 2, BLK, MY_ROWS), BF),
                vm((4, BLK, MY_ROWS), BF),
                vm((2, 8, 2, 2, MY_ROWS, HALF), BF),
                vm((2, 8, 2, MY_ROWS, HALF), BF),
                vm((2, 2, 4, 2, MY_ROWS, HALF), BF),
                vm((2, MY_ROWS, HALF), BF),
                vm((GROUPS, 4, 2, 2, PER, SLICE, BLK), BF),
                vm((GROUPS, 2, 2, PER, SLICE, BLK), BF),
                vm((GROUPS, 2, 2, 2, PER, SLICE, BLK), BF),
                vm((GROUPS, 2, 2, PER, SLICE, BLK), BF),
                vm((GROUPS, 3, PER, SLICE, BLK), BF),
                vm((GROUPS, 2, 2, 4, PER, SLICE, BLK), BF),
                vm((GROUPS, 2, 2, PER, SLICE, BLK), BF),
                vm((GROUPS, 2, 4, PER, SLICE, BLK), BF),
                vm((GROUPS, 4, PER, SLICE, BLK), BF),
                vm((GROUPS, 3, PER, SLICE, BLK), BF),
                dma((6,)),
                dma((3,)), dma((3,)),
                dma((2, 2, 4, 2)), dma((2, 2, 4, 2)),
                dma((2, 8)), dma((2, 8)),
                dma((2, 4)), dma((2, 4)),
                dma((2, 8)), dma((2, 8)),
                dma((2, 2, 4, 2)), dma((2, 2, 4, 2)),
                dma((2,)), dma((2,)),
                dma((4, GROUPS, 4)), dma((4, GROUPS, 4)),
            ],
            compiler_params=pltpu.CompilerParams(
                collective_id=0, has_side_effects=True, vmem_limit_bytes=58 << 20
            ),
            name="sparse_feed_forward",
        )(
        tokens, cotangent, up_tiles, down_tiles, up_rows, up_columns, up_counts,
        down_rows, down_columns, down_counts,
    )
    return tuple(
        pl.pallas_call(
            hand_over,
            out_shape=shapes,
            in_specs=[in_vmem] * 4,
            out_specs=(in_vmem,) * 4,
            name="hand_over",
        )(*made)
    )


def solution(mesh):
    return jax.shard_map(
        local,
        mesh=mesh,
        in_specs=(
            P("dp", "mp"),
            P("dp", "mp"),
            P("mp", None, None),
            P("mp"),
            P("mp"),
            P("mp"),
            P("mp", None, None),
            P("mp"),
            P("mp"),
            P("mp"),
        ),
        out_specs=(P("dp", "mp"), P("dp", "mp"), P("mp", "dp", None), P("mp", "dp", None)),
        check_vma=False,
    )
```

time: 118 us -> 111 us (0.941)
  local copies, waits for them, and re-layouts: 7.75 us -> 0 us
  Pallas kernels: 107 us -> 109 us
    unnamed x6 -> x0, local copies, waits for them, and re-layouts: 5.8 us -> none
    another operation x7 -> x0, local copies, waits for them, and re-layouts: 1.95 us -> none  [local(): jnp.stack([jnp.pad(v, (0, 128 - v.shape[0])) for v in (up_table, down_tab...]
    pallas_call x1 -> x2, Pallas kernels: 107 us -> 109 us  [the longest x1 106 us: local(): pl.pallas_call(kernel, out_shape=shapes, in_specs=[any_space] * 4 + [pl.B...]
where the time goes in v2:
time: 111 us; the launch traced here: 110 us
  Pallas kernels  109 us (98%)
  between operations  1.93 us (2%)
    pallas_call x1, Pallas kernels, local(): pl.pallas_call(kernel, out_shape=shapes, in_specs=[any_space] * 4 + [pl.B...  106 us
    pallas_call x1, Pallas kernels, local(): pl.pallas_call(hand_over, out_shape=shapes, in_specs=[in_vmem] * 4, out_s...  2.34 us

profile of v2, /device:TPU:8, one launch (start us, length us, event | category | flops | bytes accessed | tf_op | source)
XLA Modules:
  0.0 110.5 jit_solution(11073497565401753027)
XLA Ops:
  1.9 106.2 %sparse_feed_forward.1 = (bf16[768,128]{1,0:T(8,128)(2,1)}, bf16[768,128]{1,0:T(8,128)(2,1)}, f32[12,32,256]{2,1,0:T(8,128)}, f32[12,32,256]{2,1,0:T(8,128)}) custom-call(bf16[768,128]{1,0:T(8,128)(2,1)} %tok_in.1, bf16[768,128]{1,0:T(8,128)(2,1)} %cot_in.1, bf16[12,256,256]{2,1,0:T(8,128)(2,1)} %up_in.1, bf16[12,256,256]{2,1,0:T(8,128)(2,1)} %dn_in.1, ...), custom_call_target="tpu_custom_call" | custom-call | tf_op jit(solution)/shard_map/sparse_feed_forward/pallas_call | solution.py:556
  108.1 2.3 %hand_over.1 = (bf16[768,128]{1,0:T(8,128)(2,1)}, bf16[768,128]{1,0:T(8,128)(2,1)}, f32[12,32,256]{2,1,0:T(8,128)}, f32[12,32,256]{2,1,0:T(8,128)}) custom-call(bf16[768,128]{1,0:T(8,128)(2,1)} %get-tuple-element.8.refs_0_, bf16[768,128]{1,0:T(8,128)(2,1)} %get-tuple-element.9.refs_1_, f32[12,32,256]{2,1,0:T(8,128)} %get-tuple-element.10.refs_2_, ...), custom_call_target="tpu_custom_call" | custom-call | tf_op jit(solution)/shard_map/hand_over/pallas_call | solution.py:606

commit v3 on v2

--- a/solution.py
+++ b/solution.py
@@ -16,6 +16,7 @@
 GROUPS = 3
 PER = SLOTS // GROUPS
 SLICE = 32
+AT_ONCE = 4
 MESH = pl.DeviceIdType.MESH
 BF = jnp.bfloat16
 F32 = jnp.float32
@@ -363,14 +364,15 @@
         arrived(ref, g_s.at[kind, g, i], g_r.at[kind, g, i])
 
     def down_group(g):
-        def one(t, carry):
-            p, i = t // PER, lax.rem(t, PER)
-            out = grad_product(1, p, g * PER + i)
-            for part in range(8):
-                gd[g, part % 4, part // 4, p, i] = out[part * SLICE:(part + 1) * SLICE]
+        def some(t, carry):
+            for n in range(AT_ONCE):
+                p, i = n % 2, t * (AT_ONCE // 2) + n // 2
+                out = grad_product(1, p, g * PER + i)
+                for part in range(8):
+                    gd[g, part % 4, part // 4, p, i] = out[part * SLICE:(part + 1) * SLICE]
             return carry
 
-        lax.fori_loop(0, 2 * PER, one, 0)
+        lax.fori_loop(0, 2 * PER // AT_ONCE, some, 0)
         grad_send(0, g, 0, gd.at[g, y_next2, 0], gda.at[g, 0], y_peers[0])
         grad_send(0, g, 1, gd.at[g, y_next2, 1], gda.at[g, 1], y_peers[2])
 
@@ -382,14 +384,15 @@
             grad_send(0, g, 2 + i, gd.at[g, to], gdr.at[g, i], dev)
 
     def up_group(g):
-        def one(t, carry):
-            p, i = t // PER, lax.rem(t, PER)
-            out = grad_product(0, p, g * PER + i)
-            for part in range(8):
-                gu[g, part // 4, p, part % 4, i] = out[part * SLICE:(part + 1) * SLICE]
+        def some(t, carry):
+            for n in range(AT_ONCE):
+                p, i = n % 2, t * (AT_ONCE // 2) + n // 2
+                out = grad_product(0, p, g * PER + i)
+                for part in range(8):
+                    gu[g, part // 4, p, part % 4, i] = out[part * SLICE:(part + 1) * SLICE]
             return carry
 
-        lax.fori_loop(0, 2 * PER, one, 0)
+        lax.fori_loop(0, 2 * PER // AT_ONCE, some, 0)
         low, high = pl.ds(0, 2), pl.ds(2, 2)
         grad_send(1, g, 0, gu.at[g, flip_hi, 0, low], gua.at[g, 0], x_up)
         grad_send(1, g, 1, gu.at[g, flip_hi, 0, high], gua.at[g, 1], x_down)

time: 111 us -> 107 us (0.964)
  Pallas kernels: 109 us -> 105 us
    pallas_call x1, Pallas kernels: 106 us -> 103 us  [local(): pl.pallas_call(kernel, out_shape=shapes, in_specs=[any_space] * 4 + [pl.B...]
where the time goes in v3:
time: 107 us
  Pallas kernels  105 us (98%)
  between operations  1.93 us (2%)
    pallas_call x1, Pallas kernels, local(): pl.pallas_call(kernel, out_shape=shapes, in_specs=[any_space] * 4 + [pl.B...  103 us
    pallas_call x1, Pallas kernels, local(): pl.pallas_call(hand_over, out_shape=shapes, in_specs=[in_vmem] * 4, out_s...  2.34 us

profile of v3, /device:TPU:8, one launch (start us, length us, event | category | flops | bytes accessed | tf_op | source)
XLA Modules:
  0.0 107.3 jit_solution(7209920297817272651)
XLA Ops:
  1.9 103.0 %sparse_feed_forward.1 = (bf16[768,128]{1,0:T(8,128)(2,1)}, bf16[768,128]{1,0:T(8,128)(2,1)}, f32[12,32,256]{2,1,0:T(8,128)}, f32[12,32,256]{2,1,0:T(8,128)}) custom-call(bf16[768,128]{1,0:T(8,128)(2,1)} %tok_in.1, bf16[768,128]{1,0:T(8,128)(2,1)} %cot_in.1, bf16[12,256,256]{2,1,0:T(8,128)(2,1)} %up_in.1, bf16[12,256,256]{2,1,0:T(8,128)(2,1)} %dn_in.1, ...), custom_call_target="tpu_custom_call" | custom-call | tf_op jit(solution)/shard_map/sparse_feed_forward/pallas_call | solution.py:559
  104.9 2.3 %hand_over.1 = (bf16[768,128]{1,0:T(8,128)(2,1)}, bf16[768,128]{1,0:T(8,128)(2,1)}, f32[12,32,256]{2,1,0:T(8,128)}, f32[12,32,256]{2,1,0:T(8,128)}) custom-call(bf16[768,128]{1,0:T(8,128)(2,1)} %get-tuple-element.8.refs_0_, bf16[768,128]{1,0:T(8,128)(2,1)} %get-tuple-element.9.refs_1_, f32[12,32,256]{2,1,0:T(8,128)} %get-tuple-element.10.refs_2_, ...), custom_call_target="tpu_custom_call" | custom-call | tf_op jit(solution)/shard_map/hand_over/pallas_call | solution.py:609

commit v4 on v3

--- a/solution.py
+++ b/solution.py
@@ -225,13 +225,8 @@
             accumulate(a, 0, r, r == 0)
 
     def other_products(a):
-        accumulate(a, 1, 0, True)
-
-        def rest(r, carry):
-            accumulate(a, 1, r, False)
-            return carry
-
-        lax.fori_loop(1, 8, rest, 0)
+        for r in range(8):
+            accumulate(a, 1, r, r == 0)
 
     def gelu_step(i, carry):
         h = i // 6

time: 107 us -> 106 us (level)
    pallas_call x1, Pallas kernels: 103 us -> 102 us  [local(): pl.pallas_call(kernel, out_shape=shapes, in_specs=[any_space] * 4 + [pl.B...]
where the time goes in v4:
time: 106 us
  Pallas kernels  104 us (98%)
  between operations  1.93 us (2%)
    pallas_call x1, Pallas kernels, local(): pl.pallas_call(kernel, out_shape=shapes, in_specs=[any_space] * 4 + [pl.B...  102 us
    pallas_call x1, Pallas kernels, local(): pl.pallas_call(hand_over, out_shape=shapes, in_specs=[in_vmem] * 4, out_s...  2.34 us

profile of v4, /device:TPU:8, one launch (start us, length us, event | category | flops | bytes accessed | tf_op | source)
XLA Modules:
  0.0 106.1 jit_solution(1111206130822398164)
XLA Ops:
  1.9 101.9 %sparse_feed_forward.1 = (bf16[768,128]{1,0:T(8,128)(2,1)}, bf16[768,128]{1,0:T(8,128)(2,1)}, f32[12,32,256]{2,1,0:T(8,128)}, f32[12,32,256]{2,1,0:T(8,128)}) custom-call(bf16[768,128]{1,0:T(8,128)(2,1)} %tok_in.1, bf16[768,128]{1,0:T(8,128)(2,1)} %cot_in.1, bf16[12,256,256]{2,1,0:T(8,128)(2,1)} %up_in.1, bf16[12,256,256]{2,1,0:T(8,128)(2,1)} %dn_in.1, ...), custom_call_target="tpu_custom_call" | custom-call | tf_op jit(solution)/shard_map/sparse_feed_forward/pallas_call | solution.py:554
  103.8 2.3 %hand_over.1 = (bf16[768,128]{1,0:T(8,128)(2,1)}, bf16[768,128]{1,0:T(8,128)(2,1)}, f32[12,32,256]{2,1,0:T(8,128)}, f32[12,32,256]{2,1,0:T(8,128)}) custom-call(bf16[768,128]{1,0:T(8,128)(2,1)} %get-tuple-element.8.refs_0_, bf16[768,128]{1,0:T(8,128)(2,1)} %get-tuple-element.9.refs_1_, f32[12,32,256]{2,1,0:T(8,128)} %get-tuple-element.10.refs_2_, ...), custom_call_target="tpu_custom_call" | custom-call | tf_op jit(solution)/shard_map/hand_over/pallas_call | solution.py:604
